TPU v7x, 32 devices: a whole 2x2x4 slice. The times are simulated.
32 devices in a mesh: gx: 2 (over y), gy: 4 (over z), gz: 4 (over x, core).
Axes of the slice: x: 2, y: 2, z: 4, core: 2. Of those that a mesh axis runs over, the one named last changes fastest.
Arguments:
- inputs: bfloat16 [32, 8, 64, 512], P(None, 'gx', 'gy', 'gz'), may hold values from -6 to 6
- pre_first: bfloat16 [32, 8, 64, 512], P(None, 'gx', 'gy', 'gz'), may hold values from -6 to 6
- pre_second: bfloat16 [32, 8, 64, 512], P(None, 'gx', 'gy', 'gz'), may hold values from -6 to 6
- cotangent: bfloat16 [32, 8, 64, 512], P(None, 'gx', 'gy', 'gz'), may hold values from -6 to 6
- weight_first: bfloat16 [27, 32, 32], replicated, may hold values from -0.21875 to 0.21875
- weight_second: bfloat16 [27, 32, 32], replicated, may hold values from -0.21875 to 0.21875
Outputs:
- grad_inputs: bfloat16 [32, 8, 64, 512], P(None, 'gx', 'gy', 'gz')
- grad_first: float32 [27, 32, 32], replicated
- grad_second: float32 [27, 32, 32], replicated
All inputs are finite; a program needn't handle non-finite values.
Results may differ from a plain program's by a relative error of at most 0.005.
Values may be sent and summed in bfloat16 or wider, within the bound.
A program may use at most 128 MiB of HBM per device.

v0:
```python
import math

import jax
import jax.numpy as jnp
from jax import lax
from jax.experimental import pallas as pl
from jax.experimental.pallas import tpu as pltpu
from jax.sharding import PartitionSpec as P

MESH = pl.DeviceIdType.MESH
BF = jnp.bfloat16
F32 = jnp.float32


def exchange(k, e, faces_out, faces_in, send, recv):
    rows, _, cols, ch, nz = e.shape
    flat = cols * ch

    def axis_stage(axis, slot, up_src, up_dst, down_src, down_dst):
        me, n = lax.axis_index(axis), lax.axis_size(axis)
        has_up, has_down = me < n - 1, me > 0
        up = pltpu.make_async_remote_copy(
            up_src, up_dst, send.at[k, slot], recv.at[k, slot],
            device_id={axis: jnp.minimum(me + 1, n - 1)}, device_id_type=MESH)
        down = pltpu.make_async_remote_copy(
            down_src, down_dst, send.at[k, slot + 1], recv.at[k, slot + 1],
            device_id={axis: jnp.maximum(me - 1, 0)}, device_id_type=MESH)

        def start():
            @pl.when(has_up)
            def _():
                up.start()

            @pl.when(has_down)
            def _():
                down.start()

            @pl.when(jnp.logical_not(has_down))
            def _():
                up_dst[...] = jnp.zeros(up_dst.shape, up_dst.dtype)

            @pl.when(jnp.logical_not(has_up))
            def _():
                down_dst[...] = jnp.zeros(down_dst.shape, down_dst.dtype)

        def wait():
            @pl.when(has_up)
            def _():
                up.wait_send()
                down.wait_recv()

            @pl.when(has_down)
            def _():
                down.wait_send()
                up.wait_recv()

        return start, wait

    inner = pl.ds(1, rows - 2)
    x_start, x_wait = axis_stage(
        "gx", 0, e.at[inner, 1, cols - 2], e.at[inner, 1, 0],
        e.at[inner, 1, 1], e.at[inner, 1, cols - 1])
    y_start, y_wait = axis_stage(
        "gy", 2, e.at[rows - 2, 1], e.at[0, 1], e.at[1, 1], e.at[rows - 1, 1])
    z_start, z_wait = axis_stage(
        "gz", 4, faces_out.at[k, 0], faces_in.at[k, 0],
        faces_out.at[k, 1], faces_in.at[k, 1])

    def pack():
        r = lax.broadcasted_iota(jnp.int32, (64, nz), 0)
        lane = lax.broadcasted_iota(jnp.int32, (64, nz), 1)

        def step(y, total):
            pick = ((r == y) & (lane == nz - 1)) | ((r == y + 32) & (lane == 0))
            plane = e[y, 1].reshape(flat, nz)
            return total + lax.dot_general(
                jnp.where(pick, 1.0, 0.0).astype(BF), plane,
                (((1,), (1,)), ((), ())), preferred_element_type=F32)

        total = lax.fori_loop(0, rows, step, jnp.zeros((64, flat), F32))
        faces_out[k, 0] = total[:32].astype(BF)
        faces_out[k, 1] = total[32:].astype(BF)

    def unpack():
        kk = lax.broadcasted_iota(jnp.int32, (2 * nz, 2 * nz), 0)
        nn = lax.broadcasted_iota(jnp.int32, (2 * nz, 2 * nz), 1)
        own = kk < nz
        left = (nn < nz) & ((own & (kk == nn - 1))
                            | ((nn == 0) & (kk >= nz) & (kk < nz + 32)))
        right = (nn >= nz) & ((own & (kk == nn - nz + 1))
                              | ((nn == 2 * nz - 1) & (kk >= nz + 32) & (kk < nz + 64)))
        shift = jnp.where(left | right, 1.0, 0.0).astype(BF)
        got = jnp.concatenate([faces_in[k, 0], faces_in[k, 1]], 0).astype(F32)
        got = jnp.concatenate([got, jnp.zeros((nz - 64, flat), F32)], 0)
        got = jnp.concatenate([got, jnp.zeros((nz, 256 - flat), F32)], 1)
        columns = got.T[:flat]
        lane = lax.broadcasted_iota(jnp.int32, (flat, nz), 1)

        def step(y, _):
            mine = jnp.where((lane == y) | (lane == y + 32), columns, 0.0).astype(BF)
            plane = e[y, 1].reshape(flat, nz)
            out = jnp.dot(jnp.concatenate([plane, mine], 1), shift,
                          preferred_element_type=F32).astype(BF)
            e[y, 0] = out[:, :nz].reshape(cols, ch, nz)
            e[y, 2] = out[:, nz:].reshape(cols, ch, nz)
            return 0

        lax.fori_loop(0, rows, step, 0)

    return x_start, x_wait, y_start, y_wait, pack, z_start, z_wait, unpack


def banded(t_ref, w_ref, nx):
    ch = w_ref.shape[1]
    t_ref[...] = jnp.zeros(t_ref.shape, BF)
    for x in range(nx):
        for tap in range(27):
            ra, rb, rc = 2 - tap // 9, 2 - tap // 3 % 3, 2 - tap % 3
            col = ((rb * 3 + rc) * (nx + 2) + x + ra) * ch
            t_ref[x * ch:(x + 1) * ch, col:col + ch] = w_ref[tap]


def pair(e, y):
    _, three, cols, ch, nz = e.shape
    depth = 3 * three * cols * ch
    return jnp.concatenate([e[pl.ds(y, 3)].reshape(depth, nz),
                            e[pl.ds(y + 1, 3)].reshape(depth, nz)], 1)


def conv(e, t_ref, sink):
    ny, nz = e.shape[0] - 2, e.shape[-1]

    def step(j, _):
        y = 2 * j
        out = jnp.dot(t_ref[...], pair(e, y), preferred_element_type=F32)
        sink(y, out[:, :nz])
        sink(y + 1, out[:, nz:])
        return 0

    lax.fori_loop(0, ny // 2, step, 0)


def gram(e, a_ref, relu, acc, out_ref, which):
    ny, nx, ch, nz = a_ref.shape
    acc[...] = jnp.zeros(acc.shape, F32)

    def step(j, _):
        y = 2 * j
        a = jnp.concatenate([a_ref[y].reshape(nx * ch, nz), a_ref[y + 1].reshape(nx * ch, nz)], 1)
        if relu:
            a = jnp.maximum(a, jnp.zeros_like(a))
        acc[...] += lax.dot_general(a, pair(e, y), (((1,), (1,)), ((), ())),
                                    preferred_element_type=F32)
        return 0

    lax.fori_loop(0, ny // 2, step, 0)
    for m in range(9):
        base = m * (nx + 2) * ch
        total = acc[0:ch, base:base + 3 * ch]
        for x in range(1, nx):
            total = total + acc[x * ch:(x + 1) * ch, base + x * ch:base + (x + 3) * ch]
        out_ref[which, m, :, :3 * ch] = total
        out_ref[which, m, :, 3 * ch:] = jnp.zeros((ch, 128 - 3 * ch), F32)


def kernel(d2, p1, inp, w1, w2, gin, grads, e2, e1, t2, t1, acc, faces_out, faces_in, send, recv):
    ny, nx, ch, nz = d2.shape
    barrier = pltpu.get_barrier_semaphore()
    for axis in ("gx", "gy", "gz"):
        me, n = lax.axis_index(axis), lax.axis_size(axis)

        @pl.when(me > 0)
        def _():
            pl.semaphore_signal(barrier, inc=1, device_id={axis: jnp.maximum(me - 1, 0)},
                                device_id_type=MESH)

        @pl.when(me < n - 1)
        def _():
            pl.semaphore_signal(barrier, inc=1, device_id={axis: jnp.minimum(me + 1, n - 1)},
                                device_id_type=MESH)

    e2[pl.ds(1, ny), 1, pl.ds(1, nx)] = d2[...]
    neighbours = 0
    for axis in ("gx", "gy", "gz"):
        me, n = lax.axis_index(axis), lax.axis_size(axis)
        neighbours = neighbours + (me > 0).astype(jnp.int32) + (me < n - 1).astype(jnp.int32)
    pl.semaphore_wait(barrier, neighbours)

    stages = exchange(0, e2, faces_out, faces_in, send, recv)
    x_start, x_wait, y_start, y_wait, pack, z_start, z_wait, unpack = stages
    x_start()
    banded(t2, w2, nx)
    x_wait()
    y_start()
    banded(t1, w1, nx)
    y_wait()
    pack()
    z_start()
    z_wait()
    unpack()

    def masked(y, value):
        keep = p1[y].reshape(nx * ch, nz).astype(F32) > 0
        e1[y + 1, 1, pl.ds(1, nx)] = jnp.where(keep, value, 0.0).astype(BF).reshape(nx, ch, nz)

    conv(e2, t2, masked)
    stages = exchange(1, e1, faces_out, faces_in, send, recv)
    x_start, x_wait, y_start, y_wait, pack, z_start, z_wait, unpack = stages
    x_start()
    x_wait()
    y_start()
    y_wait()
    pack()
    z_start()
    gram(e2, p1, True, acc, grads, 1)
    z_wait()
    unpack()
    gram(e1, inp, False, acc, grads, 0)

    def rounded(y, value):
        gin[y] = value.astype(BF).reshape(nx, ch, nz)

    conv(e1, t1, rounded)


def local(inputs, pre_first, pre_second, cotangent, weight_first, weight_second):
    ch, nx, ny, nz = inputs.shape
    cells = nx * ny * nz * lax.axis_size("gx") * lax.axis_size("gy") * lax.axis_size("gz")
    scale = 1.0 / math.sqrt(cells)
    order = (2, 1, 0, 3)
    delta_two = jnp.where(pre_second > 0, cotangent, jnp.zeros_like(cotangent))
    d2, p1, inp = (jnp.transpose(v, order) for v in (delta_two, pre_first, inputs))
    vmem = pl.BlockSpec(memory_space=pltpu.VMEM)
    depth = 9 * (nx + 2) * ch
    brick = (ny + 2, 3, nx + 2, ch, nz)
    gin, grads = pl.pallas_call(
        kernel,
        out_shape=(jax.ShapeDtypeStruct((ny, nx, ch, nz), BF),
                   jax.ShapeDtypeStruct((2, 9, ch, 128), F32)),
        in_specs=[vmem] * 5,
        out_specs=(vmem, vmem),
        scratch_shapes=[
            pltpu.VMEM(brick, BF),
            pltpu.VMEM(brick, BF),
            pltpu.VMEM((nx * ch, depth), BF),
            pltpu.VMEM((nx * ch, depth), BF),
            pltpu.VMEM((nx * ch, depth), F32),
            pltpu.VMEM((2, 2, 32, (nx + 2) * ch), BF),
            pltpu.VMEM((2, 2, 32, (nx + 2) * ch), BF),
            pltpu.SemaphoreType.DMA((2, 6)),
            pltpu.SemaphoreType.DMA((2, 6)),
        ],
        compiler_params=pltpu.CompilerParams(
            collective_id=0, has_side_effects=True, vmem_limit_bytes=48 * 2**20),
    )(d2, p1, inp, weight_first, weight_second)
    total = lax.psum(grads, ("gx", "gy", "gz")) * scale
    total = total[..., :3 * ch].reshape(2, 3, 3, ch, 3, ch)
    total = jnp.flip(jnp.transpose(total, (0, 4, 1, 2, 3, 5)), (1, 2, 3)).reshape(2, 27, ch, ch)
    return jnp.transpose(gin, order), total[0], total[1]


def solution(mesh):
    cells = P(None, "gx", "gy", "gz")
    return jax.shard_map(local, mesh=mesh, in_specs=(cells,) * 4 + (P(), P()),
                         out_specs=(cells, P(), P()), check_vma=False)
```

profile of v0, /device:TPU:0, one launch (start us, length us, event | category | flops | bytes accessed | tf_op | source)
XLA Modules:
  0.0 196.4 jit_solution(2919497330471426303)
XLA Ops:
  7.2 0.0 copy-start.2
  7.2 0.0 copy-start.3
  7.2 0.0 all-reduce.2.cloned.1.call-start
  7.2 1.5 copy.32
  8.7 0.0 copy-done.2
  8.7 0.0 copy-done.3
  8.7 0.0 copy-start
  8.7 0.0 copy-start.1
  8.7 3.3 %fusion = (bf16[16,4,32,128]{3,2,1,0:T(8,128)(2,1)S(1)}, bf16[16,4,32,128]{3,2,1,0:T(8,128)(2,1)S(1)}) fusion(bf16[32,4,16,128]{3,2,1,0:T(8,128)(2,1)S(1)} %copy-done.2, bf16[32,4,16,128]{3,2,1,0:T(8,128)(2,1)S(1)} %copy-done.3, bf16[32,4,16,128]{3,2,1,0:T(8,128)(2,1)} %param.6), kind=kLoop, calls=%fused_computation.1 | loop fusion | flops 524288 | bytes 2621440 | tf_op jit(solution)/shard_map/transpose | solution.py:232
  12.1 0.0 copy-done
  12.1 0.0 copy-done.1
  12.1 46.8 %shard_map.85 = (bf16[16,4,32,128]{3,2,1,0:T(8,128)(2,1)S(1)}, f32[2,9,32,128]{3,2,1,0:T(8,128)}) custom-call(bf16[16,4,32,128]{3,2,1,0:T(8,128)(2,1)S(1)} %get-tuple-element.18.d2, bf16[16,4,32,128]{3,2,1,0:T(8,128)(2,1)S(1)} %bitcast.13, bf16[16,4,32,128]{3,2,1,0:T(8,128)(2,1)S(1)} %get-tuple-element.19.inp, bf16[27,32,32]{2,1,0:T(8,128)(2,1)S(1)} %copy-done, ...), custom_call_target="tpu_custom_call" | custom-call | tf_op jit(solution)/shard_map/pallas_call | solution.py:236
  58.9 0.0 all-reduce.2.cloned.1.call-update
  58.9 1.1 copy.27
  60.0 123.9 %all-reduce.2.cloned.1.call-done = f32[2,9,32,128]{3,2,1,0:T(8,128)} async-done(((f32[2,9,32,128]{3,2,1,0:T(8,128)}), f32[2,9,32,128]{3,2,1,0:T(8,128)}) %all-reduce.2.cloned.1.call-update) | async-done | bytes 294928 | tf_op jit(solution)/shard_map/psum | solution.py:256
  183.9 1.0 slice_multiply_fusion
  184.9 0.4 reshape.14
  185.3 0.3 fusion.1
  185.6 1.1 slice.21
  186.8 0.8 copy.26
  187.6 1.1 slice.19
  188.7 0.8 copy.25
Async XLA Ops:
  7.2 1.5 copy-start.2
  7.2 1.5 copy-start.3
  7.2 176.7 %all-reduce.2.cloned.1.call-start = ((), (), s32[]{:S(2)}) async-start(), calls=%async_computation | async-start | bytes 589824 | tf_op jit(solution)/shard_map/psum | solution.py:256
  8.7 3.4 %copy-start = (bf16[27,32,32]{2,1,0:T(8,128)(2,1)S(1)}, bf16[27,32,32]{2,1,0:T(8,128)(2,1)}, u32[]{:S(2)}) copy-start(bf16[27,32,32]{2,1,0:T(8,128)(2,1)} %w1.1) | copy-start | bytes 165892
  8.7 3.4 %copy-start.1 = (bf16[27,32,32]{2,1,0:T(8,128)(2,1)S(1)}, bf16[27,32,32]{2,1,0:T(8,128)(2,1)}, u32[]{:S(2)}) copy-start(bf16[27,32,32]{2,1,0:T(8,128)(2,1)} %w2.1) | copy-start | bytes 165892
Sparse Core Ops, SparseCore 0:
  59.0 124.8 all-reduce.1
where the time goes:
time: 197 us; the launch traced here: 196 us
  waiting for transfers between devices  124 us (63%)
  Pallas kernels  46.8 us (24%)
  between operations  14.1 us (7%)
  local copies, waits for them, and re-layouts  7.23 us (4%)
  other arithmetic  4.31 us (2%)
    psum x1, waiting for transfers between devices, local(): total = lax.psum(grads, ('gx', 'gy', 'gz')) * scale  124 us
    pallas_call x1, Pallas kernels, local(): pl.pallas_call(kernel, out_shape=(jax.ShapeDtypeStruct((ny, nx, ch, nz),...  46.8 us
    slice x5, local copies, waits for them, and re-layouts, local(): return (jnp.transpose(gin, order), total[0], total[1])  4.19 us
  transfers between devices with their start and end apart: 1, of which 1 were waited for; matrix products, arithmetic and copies ran while one was open for 1% of the time, Pallas kernels for 0%

commit v1 on v0

--- a/solution.py
+++ b/solution.py
@@ -1,3 +1,4 @@
+import functools
 import math
 
 import jax
@@ -127,7 +128,7 @@
                             e[pl.ds(y + 1, 3)].reshape(depth, nz)], 1)
 
 
-def conv(e, t_ref, sink):
+def conv(e, t_ref, sink, begin=0, end=None):
     ny, nz = e.shape[0] - 2, e.shape[-1]
 
     def step(j, _):
@@ -137,10 +138,11 @@
         sink(y + 1, out[:, nz:])
         return 0
 
-    lax.fori_loop(0, ny // 2, step, 0)
-
-
-def gram(e, a_ref, relu, acc, out_ref, which):
+    lax.fori_loop(begin, ny // 2 if end is None else end, step, 0)
+
+
+def gram(e, a_ref, relu, acc, part, which):
+    per = part.shape[1]
     ny, nx, ch, nz = a_ref.shape
     acc[...] = jnp.zeros(acc.shape, F32)
 
@@ -159,33 +161,59 @@
         total = acc[0:ch, base:base + 3 * ch]
         for x in range(1, nx):
             total = total + acc[x * ch:(x + 1) * ch, base + x * ch:base + (x + 3) * ch]
-        out_ref[which, m, :, :3 * ch] = total
-        out_ref[which, m, :, 3 * ch:] = jnp.zeros((ch, 128 - 3 * ch), F32)
-
-
-def kernel(d2, p1, inp, w1, w2, gin, grads, e2, e1, t2, t1, acc, faces_out, faces_in, send, recv):
+        total = jnp.concatenate([total, jnp.zeros((ch, 128 - 3 * ch), F32)], 1)
+        for i in range(ch // 8):
+            block = (which * 9 + m) * (ch // 8) + i
+            part[block // per, block % per] = total[8 * i:8 * i + 8]
+
+
+def everyone():
+    ny, nz = lax.axis_size("gy"), lax.axis_size("gz")
+    n = lax.axis_size("gx") * ny * nz
+    me = (lax.axis_index("gx") * ny + lax.axis_index("gy")) * nz + lax.axis_index("gz")
+
+    def place(k):
+        p = (me + k) % n
+        return (p // (ny * nz), p // nz % ny, p % nz)
+
+    return n, me, place
+
+
+def scatter_copy(part, got, sems, k):
+    n, me, place = everyone()
+    return pltpu.make_async_remote_copy(
+        part.at[(me + k) % n], got.at[k], sems[0].at[k], sems[1].at[k],
+        device_id=place(k), device_id_type=MESH)
+
+
+def gather_copy(whole, sems, k):
+    n, me, place = everyone()
+    return pltpu.make_async_remote_copy(
+        whole.at[me], whole.at[me], sems[2].at[k], sems[3].at[k],
+        device_id=place(k), device_id_type=MESH)
+
+
+def over_peers(act):
+    def step(k, _):
+        act(k)
+        return 0
+
+    lax.fori_loop(1, everyone()[0], step, 0)
+
+
+def kernel(d2, p1, inp, w1, w2, gin, first, second, e2, e1, t2, t1, acc, faces_out, faces_in,
+           part, got, whole, send, recv, *sems, scale):
     ny, nx, ch, nz = d2.shape
+    n, me, place = everyone()
     barrier = pltpu.get_barrier_semaphore()
-    for axis in ("gx", "gy", "gz"):
-        me, n = lax.axis_index(axis), lax.axis_size(axis)
-
-        @pl.when(me > 0)
-        def _():
-            pl.semaphore_signal(barrier, inc=1, device_id={axis: jnp.maximum(me - 1, 0)},
-                                device_id_type=MESH)
-
-        @pl.when(me < n - 1)
-        def _():
-            pl.semaphore_signal(barrier, inc=1, device_id={axis: jnp.minimum(me + 1, n - 1)},
-                                device_id_type=MESH)
-
+
+    def greet(k, _):
+        pl.semaphore_signal(barrier, inc=1, device_id=place(k), device_id_type=MESH)
+        return 0
+
+    lax.fori_loop(1, n, greet, 0)
     e2[pl.ds(1, ny), 1, pl.ds(1, nx)] = d2[...]
-    neighbours = 0
-    for axis in ("gx", "gy", "gz"):
-        me, n = lax.axis_index(axis), lax.axis_size(axis)
-        neighbours = neighbours + (me > 0).astype(jnp.int32) + (me < n - 1).astype(jnp.int32)
-    pl.semaphore_wait(barrier, neighbours)
-
+    pl.semaphore_wait(barrier, n - 1)
     stages = exchange(0, e2, faces_out, faces_in, send, recv)
     x_start, x_wait, y_start, y_wait, pack, z_start, z_wait, unpack = stages
     x_start()
@@ -212,15 +240,32 @@
     y_wait()
     pack()
     z_start()
-    gram(e2, p1, True, acc, grads, 1)
+    gram(e2, p1, True, acc, part, 1)
     z_wait()
     unpack()
-    gram(e1, inp, False, acc, grads, 0)
+    gram(e1, inp, False, acc, part, 0)
 
     def rounded(y, value):
         gin[y] = value.astype(BF).reshape(nx, ch, nz)
 
-    conv(e1, t1, rounded)
+    per = part.shape[1]
+    blocks = 2 * 9 * (ch // 8)
+    for block in range(blocks, n * per):
+        part[block // per, block % per] = jnp.zeros((8, 128), F32)
+    over_peers(lambda k: scatter_copy(part, got, sems, k).start())
+    conv(e1, t1, rounded, 0, ny // 4)
+    over_peers(lambda k: scatter_copy(part, got, sems, k).wait())
+    whole[me] = lax.fori_loop(1, n, lambda k, t: t + got[k], part[me]) * scale
+    over_peers(lambda k: gather_copy(whole, sems, k).start())
+    conv(e1, t1, rounded, ny // 4, ny // 2)
+    over_peers(lambda k: gather_copy(whole, sems, k).wait())
+    for which, out in enumerate((first, second)):
+        for m in range(9):
+            for i in range(ch // 8):
+                block = (which * 9 + m) * (ch // 8) + i
+                value = whole[block // per, block % per]
+                for ra in range(3):
+                    out[(2 - ra) * 9 + 8 - m, 8 * i:8 * i + 8, :] = value[:, ra * ch:(ra + 1) * ch]
 
 
 def local(inputs, pre_first, pre_second, cotangent, weight_first, weight_second):
@@ -233,12 +278,15 @@
     vmem = pl.BlockSpec(memory_space=pltpu.VMEM)
     depth = 9 * (nx + 2) * ch
     brick = (ny + 2, 3, nx + 2, ch, nz)
-    gin, grads = pl.pallas_call(
-        kernel,
+    n = lax.axis_size("gx") * lax.axis_size("gy") * lax.axis_size("gz")
+    per = -(-(2 * 9 * ch // 8) // n)
+    gin, first, second = pl.pallas_call(
+        functools.partial(kernel, scale=scale),
         out_shape=(jax.ShapeDtypeStruct((ny, nx, ch, nz), BF),
-                   jax.ShapeDtypeStruct((2, 9, ch, 128), F32)),
+                   jax.ShapeDtypeStruct(weight_first.shape, F32),
+                   jax.ShapeDtypeStruct(weight_second.shape, F32)),
         in_specs=[vmem] * 5,
-        out_specs=(vmem, vmem),
+        out_specs=(vmem,) * 3,
         scratch_shapes=[
             pltpu.VMEM(brick, BF),
             pltpu.VMEM(brick, BF),
@@ -247,16 +295,16 @@
             pltpu.VMEM((nx * ch, depth), F32),
             pltpu.VMEM((2, 2, 32, (nx + 2) * ch), BF),
             pltpu.VMEM((2, 2, 32, (nx + 2) * ch), BF),
+            pltpu.VMEM((n, per, 8, 128), F32),
+            pltpu.VMEM((n, per, 8, 128), F32),
+            pltpu.VMEM((n, per, 8, 128), F32),
             pltpu.SemaphoreType.DMA((2, 6)),
             pltpu.SemaphoreType.DMA((2, 6)),
-        ],
+        ] + [pltpu.SemaphoreType.DMA((n,))] * 4,
         compiler_params=pltpu.CompilerParams(
             collective_id=0, has_side_effects=True, vmem_limit_bytes=48 * 2**20),
     )(d2, p1, inp, weight_first, weight_second)
-    total = lax.psum(grads, ("gx", "gy", "gz")) * scale
-    total = total[..., :3 * ch].reshape(2, 3, 3, ch, 3, ch)
-    total = jnp.flip(jnp.transpose(total, (0, 4, 1, 2, 3, 5)), (1, 2, 3)).reshape(2, 27, ch, ch)
-    return jnp.transpose(gin, order), total[0], total[1]
+    return jnp.transpose(gin, order), first, second
 
 
 def solution(mesh):

time: 197 us -> 77.4 us (0.39)
  waiting for transfers between devices: 124 us -> 0 us
  Pallas kernels: 46.8 us -> 69 us
  between operations: 14.1 us -> 0.71 us
  local copies, waits for them, and re-layouts: 7.23 us -> 4.15 us
    psum x1 -> x0, waiting for transfers between devices: 124 us -> none  [local(): total = lax.psum(grads, ('gx', 'gy', 'gz')) * scale]
    pallas_call x1, Pallas kernels: 46.8 us -> 69 us  [local(): pl.pallas_call(functools.partial(kernel, scale=scale), out_shape=(jax.Sha...]
    slice x5 -> x0, local copies, waits for them, and re-layouts: 4.19 us -> none  [local(): return (jnp.transpose(gin, order), total[0], total[1])]
    unnamed x10 -> x12, local copies, waits for them, and re-layouts: 2.62 us -> 4.15 us
  transfers between devices with their start and end apart: 1 -> 0, of which waited for: 1 -> 0; matrix products, arithmetic and copies ran while one was open for 1% -> 0% of each run, Pallas kernels for 0% -> 0%
where the time goes in v1:
time: 77.4 us; the launch traced here: 77.2 us
  Pallas kernels  69 us (89%)
  local copies, waits for them, and re-layouts  4.15 us (5%)
  other arithmetic  3.33 us (4%)
    pallas_call x1, Pallas kernels, local(): pl.pallas_call(functools.partial(kernel, scale=scale), out_shape=(jax.Sha...  69 us
    unnamed x12, local copies, waits for them, and re-layouts  4.15 us
    transpose x1, other arithmetic, local(): jnp.transpose(v, order)  3.33 us

profile of v1, /device:TPU:0, one launch (start us, length us, event | category | flops | bytes accessed | tf_op | source)
XLA Modules:
  0.0 77.2 jit_solution(8492984599130081414)
XLA Ops:
  0.6 0.0 copy-start.2
  0.6 0.0 copy-start.3
  0.7 1.5 %copy.18 = bf16[32,4,16,128]{3,0,1,2:T(8,128)(2,1)S(1)} copy(bf16[32,4,16,128]{3,2,1,0:T(8,128)(2,1)} %param.7) | data formatting | bytes 1048576 | tf_op args[1]
  2.1 0.0 copy-done.2
  2.1 0.0 copy-done.3
  2.1 0.0 copy-start
  2.2 0.0 copy-start.1
  2.2 3.3 %fusion = (bf16[16,4,32,128]{3,2,1,0:T(8,128)(2,1)S(1)}, bf16[16,4,32,128]{3,2,1,0:T(8,128)(2,1)S(1)}) fusion(bf16[32,4,16,128]{3,2,1,0:T(8,128)(2,1)S(1)} %copy-done.2, bf16[32,4,16,128]{3,2,1,0:T(8,128)(2,1)S(1)} %copy-done.3, bf16[32,4,16,128]{3,2,1,0:T(8,128)(2,1)} %param.6), kind=kLoop, calls=%fused_computation.1 | loop fusion | flops 524288 | bytes 2621440 | tf_op jit(solution)/shard_map/transpose | solution.py:277
  5.5 0.0 copy-done
  5.5 0.0 copy-done.1
  5.5 69.0 %shard_map.85 = (bf16[16,4,32,128]{3,2,1,0:T(8,128)(2,1)S(1)}, f32[27,32,32]{2,1,0:T(8,128)S(1)}, f32[27,32,32]{2,1,0:T(8,128)S(1)}) custom-call(bf16[16,4,32,128]{3,2,1,0:T(8,128)(2,1)S(1)} %get-tuple-element.12.d2, bf16[16,4,32,128]{3,2,1,0:T(8,128)(2,1)S(1)} %bitcast.8, bf16[16,4,32,128]{3,2,1,0:T(8,128)(2,1)S(1)} %get-tuple-element.13.inp, ...), custom_call_target="tpu_custom_call" | custom-call | tf_op jit(solution)/shard_map/pallas_call | solution.py:283
  74.6 1.1 %copy.13 = bf16[32,4,16,128]{3,2,1,0:T(8,128)(2,1)} copy(bf16[32,4,16,128]{3,0,1,2:T(8,128)(2,1)S(1)} %bitcast.9) | data formatting | bytes 1048576
  75.7 0.8 copy.21
  76.5 0.8 copy.22
Async XLA Ops:
  0.6 1.5 %copy-start.2 = (bf16[32,4,16,128]{3,2,1,0:T(8,128)(2,1)S(1)}, bf16[32,4,16,128]{3,2,1,0:T(8,128)(2,1)}, u32[]{:S(2)}) copy-start(bf16[32,4,16,128]{3,2,1,0:T(8,128)(2,1)} %param.9) | copy-start | bytes 1572868
  0.6 1.5 %copy-start.3 = (bf16[32,4,16,128]{3,2,1,0:T(8,128)(2,1)S(1)}, bf16[32,4,16,128]{3,2,1,0:T(8,128)(2,1)}, u32[]{:S(2)}) copy-start(bf16[32,4,16,128]{3,2,1,0:T(8,128)(2,1)} %param.8) | copy-start | bytes 1572868
  2.1 3.4 %copy-start = (bf16[27,32,32]{2,1,0:T(8,128)(2,1)S(1)}, bf16[27,32,32]{2,1,0:T(8,128)(2,1)}, u32[]{:S(2)}) copy-start(bf16[27,32,32]{2,1,0:T(8,128)(2,1)} %w1.1) | copy-start | bytes 165892
  2.2 3.4 %copy-start.1 = (bf16[27,32,32]{2,1,0:T(8,128)(2,1)S(1)}, bf16[27,32,32]{2,1,0:T(8,128)(2,1)}, u32[]{:S(2)}) copy-start(bf16[27,32,32]{2,1,0:T(8,128)(2,1)} %w2.1) | copy-start | bytes 165892

commit v2 on v1

v2 whole, which is shorter than its diff:
```python
import functools
import math

import jax
import jax.numpy as jnp
from jax import lax
from jax.experimental import pallas as pl
from jax.experimental.pallas import tpu as pltpu
from jax.sharding import PartitionSpec as P

MESH = pl.DeviceIdType.MESH
BF = jnp.bfloat16
F32 = jnp.float32


DIRECTIONS = [(dx, dy, dz) for dz in (0, 1, -1) for dx in (0, 1, -1) for dy in (0, 1, -1)
              if (dx, dy, dz) != (0, 0, 0)]


def near(direction, sign):
    exists, place = None, []
    for axis, d in zip(("gx", "gy", "gz"), direction):
        me, n = lax.axis_index(axis), lax.axis_size(axis)
        if d:
            there = me + sign * d
            ok = (there >= 0) & (there < n)
            exists = ok if exists is None else exists & ok
            me = jnp.clip(there, 0, n - 1)
        place.append(me)
    return exists, tuple(place)


def clear_halo(e):
    rows, _, cols, ch, nz = e.shape
    for y in (0, rows - 1):
        e[y, 1] = jnp.zeros((cols, ch, nz), BF)
    for x in (0, cols - 1):
        e[pl.ds(1, rows - 2), 1, x] = jnp.zeros((rows - 2, ch, nz), BF)


def exchange(k, e, faces_out, faces_in, edge, send, recv):
    rows, _, cols, ch, nz = e.shape
    nx, ny, flat = cols - 2, rows - 2, cols * ch

    def ends(d, n):
        if d == 0:
            return pl.ds(1, n), pl.ds(1, n)
        return (n, 0) if d > 0 else (1, n + 1)

    def copy(i):
        dx, dy, dz = DIRECTIONS[i]
        if dz == 0:
            (sx, tx), (sy, ty) = ends(dx, nx), ends(dy, ny)
            src, dst = e.at[sy, 1, sx], e.at[ty, 1, tx]
        else:
            side = 0 if dz > 0 else 1
            src = faces_out.at[k, side]
            dst = faces_in.at[k, side, (dx + 1) * 3 + dy + 1]
        exists, place = near(DIRECTIONS[i], 1)
        return exists, pltpu.make_async_remote_copy(
            src, dst, send.at[k, i], recv.at[k, i], device_id=place, device_id_type=MESH)

    def start(picked):
        for i in picked:
            exists, one = copy(i)
            pl.when(exists)(one.start)

    def begin():
        start(range(8))
        r = lax.broadcasted_iota(jnp.int32, (2 * ny, 2 * nz), 0)
        lane = lax.broadcasted_iota(jnp.int32, (2 * ny, 2 * nz), 1)
        total = jnp.zeros((2 * ny, nx * ch), F32)
        for y in range(0, ny, 2):
            pick = (((r == y) & (lane == nz - 1)) | ((r == y + ny) & (lane == 0))
                    | ((r == y + 1) & (lane == 2 * nz - 1)) | ((r == y + 1 + ny) & (lane == nz)))
            planes = jnp.concatenate(
                [e[y + 1 + j, 1, pl.ds(1, nx)].reshape(nx * ch, nz) for j in (0, 1)], 1)
            total = total + lax.dot_general(
                jnp.where(pick, 1.0, 0.0).astype(BF), planes,
                (((1,), (1,)), ((), ())), preferred_element_type=F32)
        faces_out[k, 0] = total[:ny].astype(BF)
        faces_out[k, 1] = total[ny:].astype(BF)
        start(range(8, 26))

    def finish():
        for i in range(26):
            exists, one = copy(i)
            pl.when(exists)(one.wait_send)
            came, _ = near(DIRECTIONS[i], -1)
            pl.when(came)(one.wait_recv)

        kk = lax.broadcasted_iota(jnp.int32, (2 * nz, 2 * nz), 0)
        nn = lax.broadcasted_iota(jnp.int32, (2 * nz, 2 * nz), 1)
        own = kk < nz
        left = (nn < nz) & ((own & (kk == nn - 1))
                            | ((nn == 0) & (kk >= nz) & (kk < nz + 32)))
        right = (nn >= nz) & ((own & (kk == nn - nz + 1))
                              | ((nn == 2 * nz - 1) & (kk >= nz + 32) & (kk < nz + 64)))
        shift = jnp.where(left | right, 1.0, 0.0).astype(BF)
        for side in (0, 1):
            for dx in (-1, 0, 1):
                for dy in (-1, 0, 1):
                    face = faces_in[k, side, (dx + 1) * 3 + dy + 1].astype(F32)
                    at = 32 * side
                    if dy == 0:
                        ys, yt = slice(0, ny), slice(at + 1, at + 1 + ny)
                    elif dy > 0:
                        ys, yt = slice(ny - 1, ny), slice(at, at + 1)
                    else:
                        ys, yt = slice(0, 1), slice(at + ny + 1, at + ny + 2)
                    if dx == 0:
                        xs, xt = slice(0, nx * ch), slice(ch, ch + nx * ch)
                    elif dx > 0:
                        xs, xt = slice((nx - 1) * ch, nx * ch), slice(0, ch)
                    else:
                        xs, xt = slice(0, ch), slice((nx + 1) * ch, (nx + 2) * ch)
                    edge[yt, xt] = face[ys, xs]
        columns = edge[...].T[:flat]
        lane = lax.broadcasted_iota(jnp.int32, (flat, nz), 1)

        def step(j, _):
            y = 3 * j
            mine = jnp.concatenate(
                [jnp.where((lane == y + i) | (lane == y + i + 32), columns, 0.0).astype(BF)
                 for i in range(3)], 0)
            planes = e[pl.ds(y, 3), 1].reshape(3 * flat, nz)
            out = jnp.dot(jnp.concatenate([planes, mine], 1), shift,
                          preferred_element_type=F32).astype(BF)
            e[pl.ds(y, 3), 0] = out[:, :nz].reshape(3, cols, ch, nz)
            e[pl.ds(y, 3), 2] = out[:, nz:].reshape(3, cols, ch, nz)
            return 0

        lax.fori_loop(0, rows // 3, step, 0)

    return begin, finish


def banded(t_ref, w_ref, nx):
    ch = w_ref.shape[1]
    t_ref[...] = jnp.zeros(t_ref.shape, BF)
    for x in range(nx):
        for tap in range(27):
            ra, rb, rc = 2 - tap // 9, 2 - tap // 3 % 3, 2 - tap % 3
            col = ((rb * 3 + rc) * (nx + 2) + x + ra) * ch
            t_ref[x * ch:(x + 1) * ch, col:col + ch] = w_ref[tap]


def group(e, y):
    _, three, cols, ch, nz = e.shape
    depth = 3 * three * cols * ch
    return jnp.concatenate([e[pl.ds(y + i, 3)].reshape(depth, nz) for i in range(4)], 1)


def conv(e, t_ref, sink, begin, end):
    nz = e.shape[-1]

    def step(j, _):
        y = 4 * j
        out = jnp.dot(t_ref[...], group(e, y), preferred_element_type=F32)
        for i in range(4):
            sink(y + i, out[:, i * nz:(i + 1) * nz])
        return 0

    lax.fori_loop(begin, end, step, 0)


def gram(e, a_ref, relu, acc, part, which):
    per = part.shape[1]
    ny, nx, ch, nz = a_ref.shape
    acc[...] = jnp.zeros(acc.shape, F32)

    def step(j, _):
        y = 4 * j
        a = jnp.concatenate([a_ref[y + i].reshape(nx * ch, nz) for i in range(4)], 1)
        if relu:
            a = jnp.maximum(a, jnp.zeros_like(a))
        acc[...] += lax.dot_general(a, group(e, y), (((1,), (1,)), ((), ())),
                                    preferred_element_type=F32)
        return 0

    lax.fori_loop(0, ny // 4, step, 0)
    for m in range(9):
        base = m * (nx + 2) * ch
        total = acc[0:ch, base:base + 3 * ch]
        for x in range(1, nx):
            total = total + acc[x * ch:(x + 1) * ch, base + x * ch:base + (x + 3) * ch]
        for ra in range(3):
            q = (which * 9 + m) * 3 + ra
            lane = q % 4 * ch
            for h in range(ch // 16):
                block = q // 4 * (ch // 16) + h
                part[block // per, block % per, :, lane:lane + ch] = (
                    total[16 * h:16 * h + 16, ra * ch:(ra + 1) * ch])


def everyone():
    ny, nz = lax.axis_size("gy"), lax.axis_size("gz")
    n = lax.axis_size("gx") * ny * nz
    me = (lax.axis_index("gx") * ny + lax.axis_index("gy")) * nz + lax.axis_index("gz")

    def place(k):
        p = (me + k) % n
        return (p // (ny * nz), p // nz % ny, p % nz)

    return n, me, place


def scatter_copy(part, got, sems, k):
    n, me, place = everyone()
    return pltpu.make_async_remote_copy(
        part.at[(me + k) % n], got.at[k], sems[0].at[k], sems[1].at[k],
        device_id=place(k), device_id_type=MESH)


def gather_copy(whole, sems, k):
    n, me, place = everyone()
    return pltpu.make_async_remote_copy(
        whole.at[me], whole.at[me], sems[2].at[k], sems[3].at[k],
        device_id=place(k), device_id_type=MESH)


def over_peers(act):
    def step(k, _):
        act(k)
        return 0

    lax.fori_loop(1, everyone()[0], step, 0)


def kernel(d2, p1, inp, w1, w2, gin, first, second, e2, e1, t2, t1, acc, faces_out, faces_in,
           edge, part, got, whole, send, recv, *sems, scale):
    ny, nx, ch, nz = d2.shape
    n, me, place = everyone()
    clear_halo(e2)
    clear_halo(e1)
    faces_in[...] = jnp.zeros(faces_in.shape, BF)
    barrier = pltpu.get_barrier_semaphore()

    def greet(k, _):
        pl.semaphore_signal(barrier, inc=1, device_id=place(k), device_id_type=MESH)
        return 0

    lax.fori_loop(1, n, greet, 0)
    e2[pl.ds(1, ny), 1, pl.ds(1, nx)] = d2[...]
    part[...] = jnp.zeros(part.shape, F32)
    edge[...] = jnp.zeros(edge.shape, F32)
    banded(t2, w2, nx)
    pl.semaphore_wait(barrier, n - 1)
    begin, finish = exchange(0, e2, faces_out, faces_in, edge, send, recv)
    begin()
    banded(t1, w1, nx)
    finish()

    def masked(y, value):
        keep = p1[y].reshape(nx * ch, nz).astype(F32) > 0
        e1[y + 1, 1, pl.ds(1, nx)] = jnp.where(keep, value, 0.0).astype(BF).reshape(nx, ch, nz)

    conv(e2, t2, masked, 0, ny // 4)
    begin, finish = exchange(1, e1, faces_out, faces_in, edge, send, recv)
    begin()
    gram(e2, p1, True, acc, part, 1)
    finish()
    gram(e1, inp, False, acc, part, 0)

    def rounded(y, value):
        gin[y] = value.astype(BF).reshape(nx, ch, nz)

    over_peers(lambda k: scatter_copy(part, got, sems, k).start())
    conv(e1, t1, rounded, 0, ny // 8)
    over_peers(lambda k: scatter_copy(part, got, sems, k).wait())
    total = lax.fori_loop(1, n, lambda k, t: t + got[k], part[me])
    whole[me] = (total * scale).astype(BF)
    over_peers(lambda k: gather_copy(whole, sems, k).start())
    conv(e1, t1, rounded, ny // 8, ny // 4)
    over_peers(lambda k: gather_copy(whole, sems, k).wait())
    per = part.shape[1]
    for which, out in enumerate((first, second)):
        for m in range(9):
            for ra in range(3):
                q = (which * 9 + m) * 3 + ra
                lane = q % 4 * ch
                for h in range(ch // 16):
                    block = q // 4 * (ch // 16) + h
                    value = whole[block // per, block % per].astype(F32)
                    out[(2 - ra) * 9 + 8 - m, 16 * h:16 * h + 16, :] = value[:, lane:lane + ch]


def local(inputs, pre_first, pre_second, cotangent, weight_first, weight_second):
    ch, nx, ny, nz = inputs.shape
    cells = nx * ny * nz * lax.axis_size("gx") * lax.axis_size("gy") * lax.axis_size("gz")
    scale = 1.0 / math.sqrt(cells)
    order = (2, 1, 0, 3)
    delta_two = jnp.where(pre_second > 0, cotangent, jnp.zeros_like(cotangent))
    d2, p1, inp = (jnp.transpose(v, order) for v in (delta_two, pre_first, inputs))
    vmem = pl.BlockSpec(memory_space=pltpu.VMEM)
    depth = 9 * (nx + 2) * ch
    brick = (ny + 2, 3, nx + 2, ch, nz)
    n = lax.axis_size("gx") * lax.axis_size("gy") * lax.axis_size("gz")
    per = -(-(-(-2 * 27 // 4) * (ch // 16)) // n)
    gin, first, second = pl.pallas_call(
        functools.partial(kernel, scale=scale),
        out_shape=(jax.ShapeDtypeStruct((ny, nx, ch, nz), BF),
                   jax.ShapeDtypeStruct(weight_first.shape, F32),
                   jax.ShapeDtypeStruct(weight_second.shape, F32)),
        in_specs=[vmem] * 5,
        out_specs=(vmem,) * 3,
        scratch_shapes=[
            pltpu.VMEM(brick, BF),
            pltpu.VMEM(brick, BF),
            pltpu.VMEM((nx * ch, depth), BF),
            pltpu.VMEM((nx * ch, depth), BF),
            pltpu.VMEM((nx * ch, depth), F32),
            pltpu.VMEM((2, 2, ny, nx * ch), BF),
            pltpu.VMEM((2, 2, 9, ny, nx * ch), BF),
            pltpu.VMEM((nz, 256), F32),
            pltpu.VMEM((n, per, 16, 128), F32),
            pltpu.VMEM((n, per, 16, 128), F32),
            pltpu.VMEM((n, per, 16, 128), BF),
            pltpu.SemaphoreType.DMA((2, 26)),
            pltpu.SemaphoreType.DMA((2, 26)),
        ] + [pltpu.SemaphoreType.DMA((n,))] * 4,
        compiler_params=pltpu.CompilerParams(
            collective_id=0, has_side_effects=True, vmem_limit_bytes=48 * 2**20),
    )(d2, p1, inp, weight_first, weight_second)
    return jnp.transpose(gin, order), first, second


def solution(mesh):
    cells = P(None, "gx", "gy", "gz")
    return jax.shard_map(local, mesh=mesh, in_specs=(cells,) * 4 + (P(), P()),
                         out_specs=(cells, P(), P()), check_vma=False)
```

time: 77.4 us -> 50.8 us (0.66)
  Pallas kernels: 69 us -> 42.5 us
    pallas_call x1, Pallas kernels: 69 us -> 42.5 us  [local(): pl.pallas_call(functools.partial(kernel, scale=scale), out_shape=(jax.Sha...]
where the time goes in v2:
time: 50.8 us; the launch traced here: 50.7 us
  Pallas kernels  42.5 us (84%)
  local copies, waits for them, and re-layouts  4.15 us (8%)
  other arithmetic  3.33 us (7%)
  between operations  0.71 us (1%)
    pallas_call x1, Pallas kernels, local(): pl.pallas_call(functools.partial(kernel, scale=scale), out_shape=(jax.Sha...  42.5 us
    unnamed x12, local copies, waits for them, and re-layouts  4.15 us
    transpose x1, other arithmetic, local(): jnp.transpose(v, order)  3.33 us

profile of v2, /device:TPU:0, one launch (start us, length us, event | category | flops | bytes accessed | tf_op | source)
XLA Modules:
  0.0 50.7 jit_solution(15280627074613659789)
XLA Ops:
  0.6 0.0 copy-start.2
  0.6 0.0 copy-start.3
  0.7 1.5 %copy.18 = bf16[32,4,16,128]{3,0,1,2:T(8,128)(2,1)S(1)} copy(bf16[32,4,16,128]{3,2,1,0:T(8,128)(2,1)} %param.7) | data formatting | bytes 1048576 | tf_op args[1]
  2.1 0.0 copy-done.2
  2.1 0.0 copy-done.3
  2.1 0.0 copy-start
  2.2 0.0 copy-start.1
  2.2 3.3 %fusion = (bf16[16,4,32,128]{3,2,1,0:T(8,128)(2,1)S(1)}, bf16[16,4,32,128]{3,2,1,0:T(8,128)(2,1)S(1)}) fusion(bf16[32,4,16,128]{3,2,1,0:T(8,128)(2,1)S(1)} %copy-done.2, bf16[32,4,16,128]{3,2,1,0:T(8,128)(2,1)S(1)} %copy-done.3, bf16[32,4,16,128]{3,2,1,0:T(8,128)(2,1)} %param.6), kind=kLoop, calls=%fused_computation.1 | loop fusion | flops 524288 | bytes 2621440 | tf_op jit(solution)/shard_map/transpose | solution.py:294
  5.5 0.0 copy-done
  5.5 0.0 copy-done.1
  5.5 42.5 %shard_map.85 = (bf16[16,4,32,128]{3,2,1,0:T(8,128)(2,1)S(1)}, f32[27,32,32]{2,1,0:T(8,128)S(1)}, f32[27,32,32]{2,1,0:T(8,128)S(1)}) custom-call(bf16[16,4,32,128]{3,2,1,0:T(8,128)(2,1)S(1)} %get-tuple-element.12.d2, bf16[16,4,32,128]{3,2,1,0:T(8,128)(2,1)S(1)} %bitcast.8, bf16[16,4,32,128]{3,2,1,0:T(8,128)(2,1)S(1)} %get-tuple-element.13.inp, ...), custom_call_target="tpu_custom_call" | custom-call | tf_op jit(solution)/shard_map/pallas_call | solution.py:300
  48.0 1.1 %copy.13 = bf16[32,4,16,128]{3,2,1,0:T(8,128)(2,1)} copy(bf16[32,4,16,128]{3,0,1,2:T(8,128)(2,1)S(1)} %bitcast.9) | data formatting | bytes 1048576
  49.2 0.8 %copy.21 = f32[27,32,32]{2,1,0:T(8,128)} copy(f32[27,32,32]{2,1,0:T(8,128)S(1)} %get-tuple-element.18) | data formatting | bytes 221184
  49.9 0.8 %copy.22 = f32[27,32,32]{2,1,0:T(8,128)} copy(f32[27,32,32]{2,1,0:T(8,128)S(1)} %get-tuple-element.19) | data formatting | bytes 221184
Async XLA Ops:
  0.6 1.5 %copy-start.2 = (bf16[32,4,16,128]{3,2,1,0:T(8,128)(2,1)S(1)}, bf16[32,4,16,128]{3,2,1,0:T(8,128)(2,1)}, u32[]{:S(2)}) copy-start(bf16[32,4,16,128]{3,2,1,0:T(8,128)(2,1)} %param.9) | copy-start | bytes 1572868
  0.6 1.5 %copy-start.3 = (bf16[32,4,16,128]{3,2,1,0:T(8,128)(2,1)S(1)}, bf16[32,4,16,128]{3,2,1,0:T(8,128)(2,1)}, u32[]{:S(2)}) copy-start(bf16[32,4,16,128]{3,2,1,0:T(8,128)(2,1)} %param.8) | copy-start | bytes 1572868
  2.1 3.4 %copy-start = (bf16[27,32,32]{2,1,0:T(8,128)(2,1)S(1)}, bf16[27,32,32]{2,1,0:T(8,128)(2,1)}, u32[]{:S(2)}) copy-start(bf16[27,32,32]{2,1,0:T(8,128)(2,1)} %w1.1) | copy-start | bytes 165892
  2.2 3.4 %copy-start.1 = (bf16[27,32,32]{2,1,0:T(8,128)(2,1)S(1)}, bf16[27,32,32]{2,1,0:T(8,128)(2,1)}, u32[]{:S(2)}) copy-start(bf16[27,32,32]{2,1,0:T(8,128)(2,1)} %w2.1) | copy-start | bytes 165892

commit v3 on v2

--- a/solution.py
+++ b/solution.py
@@ -130,7 +130,7 @@
             e[pl.ds(y, 3), 2] = out[:, nz:].reshape(3, cols, ch, nz)
             return 0
 
-        lax.fori_loop(0, rows // 3, step, 0)
+        lax.fori_loop(0, rows // 3, step, 0, unroll=2)
 
     return begin, finish
 
@@ -161,7 +161,7 @@
             sink(y + i, out[:, i * nz:(i + 1) * nz])
         return 0
 
-    lax.fori_loop(begin, end, step, 0)
+    lax.fori_loop(begin, end, step, 0, unroll=True)
 
 
 def gram(e, a_ref, relu, acc, part, which):
@@ -178,7 +178,7 @@
                                     preferred_element_type=F32)
         return 0
 
-    lax.fori_loop(0, ny // 4, step, 0)
+    lax.fori_loop(0, ny // 4, step, 0, unroll=True)
     for m in range(9):
         base = m * (nx + 2) * ch
         total = acc[0:ch, base:base + 3 * ch]
@@ -268,7 +268,7 @@
     over_peers(lambda k: scatter_copy(part, got, sems, k).start())
     conv(e1, t1, rounded, 0, ny // 8)
     over_peers(lambda k: scatter_copy(part, got, sems, k).wait())
-    total = lax.fori_loop(1, n, lambda k, t: t + got[k], part[me])
+    total = part[me] + jnp.sum(got[1:], axis=0)
     whole[me] = (total * scale).astype(BF)
     over_peers(lambda k: gather_copy(whole, sems, k).start())
     conv(e1, t1, rounded, ny // 8, ny // 4)

time: 50.8 us -> 48.2 us (0.949)
  Pallas kernels: 42.5 us -> 39.9 us
    pallas_call x1, Pallas kernels: 42.5 us -> 39.9 us  [local(): pl.pallas_call(functools.partial(kernel, scale=scale), out_shape=(jax.Sha...]
where the time goes in v3:
time: 48.2 us; the launch traced here: 48.1 us
  Pallas kernels  39.9 us (83%)
  local copies, waits for them, and re-layouts  4.15 us (9%)
  other arithmetic  3.33 us (7%)
  between operations  0.71 us (1%)
    pallas_call x1, Pallas kernels, local(): pl.pallas_call(functools.partial(kernel, scale=scale), out_shape=(jax.Sha...  39.9 us
    unnamed x12, local copies, waits for them, and re-layouts  4.15 us
    transpose x1, other arithmetic, local(): jnp.transpose(v, order)  3.33 us

profile of v3, /device:TPU:0, one launch (start us, length us, event | category | flops | bytes accessed | tf_op | source)
XLA Modules:
  0.0 48.1 jit_solution(1901441938106544622)
XLA Ops:
  0.6 0.0 copy-start.2
  0.6 0.0 copy-start.3
  0.7 1.5 %copy.18 = bf16[32,4,16,128]{3,0,1,2:T(8,128)(2,1)S(1)} copy(bf16[32,4,16,128]{3,2,1,0:T(8,128)(2,1)} %param.7) | data formatting | bytes 1048576 | tf_op args[1]
  2.1 0.0 copy-done.2
  2.1 0.0 copy-done.3
  2.1 0.0 copy-start
  2.2 0.0 copy-start.1
  2.2 3.3 %fusion = (bf16[16,4,32,128]{3,2,1,0:T(8,128)(2,1)S(1)}, bf16[16,4,32,128]{3,2,1,0:T(8,128)(2,1)S(1)}) fusion(bf16[32,4,16,128]{3,2,1,0:T(8,128)(2,1)S(1)} %copy-done.2, bf16[32,4,16,128]{3,2,1,0:T(8,128)(2,1)S(1)} %copy-done.3, bf16[32,4,16,128]{3,2,1,0:T(8,128)(2,1)} %param.6), kind=kLoop, calls=%fused_computation.1 | loop fusion | flops 524288 | bytes 2621440 | tf_op jit(solution)/shard_map/transpose | solution.py:294
  5.5 0.0 copy-done
  5.5 0.0 copy-done.1
  5.5 39.9 %shard_map.85 = (bf16[16,4,32,128]{3,2,1,0:T(8,128)(2,1)S(1)}, f32[27,32,32]{2,1,0:T(8,128)S(1)}, f32[27,32,32]{2,1,0:T(8,128)S(1)}) custom-call(bf16[16,4,32,128]{3,2,1,0:T(8,128)(2,1)S(1)} %get-tuple-element.12.d2, bf16[16,4,32,128]{3,2,1,0:T(8,128)(2,1)S(1)} %bitcast.8, bf16[16,4,32,128]{3,2,1,0:T(8,128)(2,1)S(1)} %get-tuple-element.13.inp, ...), custom_call_target="tpu_custom_call" | custom-call | tf_op jit(solution)/shard_map/pallas_call | solution.py:300
  45.4 1.1 %copy.13 = bf16[32,4,16,128]{3,2,1,0:T(8,128)(2,1)} copy(bf16[32,4,16,128]{3,0,1,2:T(8,128)(2,1)S(1)} %bitcast.9) | data formatting | bytes 1048576
  46.5 0.8 %copy.21 = f32[27,32,32]{2,1,0:T(8,128)} copy(f32[27,32,32]{2,1,0:T(8,128)S(1)} %get-tuple-element.18) | data formatting | bytes 221184
  47.3 0.8 %copy.22 = f32[27,32,32]{2,1,0:T(8,128)} copy(f32[27,32,32]{2,1,0:T(8,128)S(1)} %get-tuple-element.19) | data formatting | bytes 221184
Async XLA Ops:
  0.6 1.5 %copy-start.2 = (bf16[32,4,16,128]{3,2,1,0:T(8,128)(2,1)S(1)}, bf16[32,4,16,128]{3,2,1,0:T(8,128)(2,1)}, u32[]{:S(2)}) copy-start(bf16[32,4,16,128]{3,2,1,0:T(8,128)(2,1)} %param.9) | copy-start | bytes 1572868
  0.6 1.5 %copy-start.3 = (bf16[32,4,16,128]{3,2,1,0:T(8,128)(2,1)S(1)}, bf16[32,4,16,128]{3,2,1,0:T(8,128)(2,1)}, u32[]{:S(2)}) copy-start(bf16[32,4,16,128]{3,2,1,0:T(8,128)(2,1)} %param.8) | copy-start | bytes 1572868
  2.1 3.4 %copy-start = (bf16[27,32,32]{2,1,0:T(8,128)(2,1)S(1)}, bf16[27,32,32]{2,1,0:T(8,128)(2,1)}, u32[]{:S(2)}) copy-start(bf16[27,32,32]{2,1,0:T(8,128)(2,1)} %w1.1) | copy-start | bytes 165892
  2.2 3.4 %copy-start.1 = (bf16[27,32,32]{2,1,0:T(8,128)(2,1)S(1)}, bf16[27,32,32]{2,1,0:T(8,128)(2,1)}, u32[]{:S(2)}) copy-start(bf16[27,32,32]{2,1,0:T(8,128)(2,1)} %w2.1) | copy-start | bytes 165892
